TPU v7x, 512 devices: a whole 4x8x8 slice. The times are simulated.
512 devices in a mesh: gx: 2 (over core), yz: 64 (over x, z, y_hi), ta: 4 (over y_lo).
Axes of the slice: x: 4, y: 8 (y_hi: 2, y_lo: 4; y = y_hi * 4 + y_lo), z: 8, core: 2. Of those that a mesh axis runs over, the one named last changes fastest.
Arguments:
- snapshot: bfloat16 [1024, 512, 8, 256], P('gx', 'yz', 'ta'), may hold values from -6144 to 6144
- y_factor: bfloat16 [512, 256], P('yz'), may hold values from -0.5 to 2.5
- z_factor: bfloat16 [256, 256], P('yz'), may hold values from -0.5 to 2.5
- t_factor: bfloat16 [8, 256], P('ta'), may hold values from -0.5 to 2.5
Outputs:
- x_factor: float32 [1024, 256], P(('gx', 'yz', 'ta'))
All inputs are finite; a program needn't handle non-finite values.
Results may differ from a plain program's by a relative error of at most 0.0003.
Values may be sent and summed in bfloat16 or wider, within the bound.
No kernel may reach another device: no remote copies, remote signals or barrier semaphores. Data moves between devices by JAX's collectives and lax.ppermute only.
A program may use at most 64 MiB of HBM per device.

v0:
```python
import jax
import jax.numpy as jnp
from jax import lax
from jax.sharding import PartitionSpec as P


def per_device(snapshot, y_factor, z_factor, t_factor):
    whole_z = lax.all_gather(z_factor, "yz", axis=0, tiled=True)
    rows_x, cols_y, cols_t, cells_z = snapshot.shape
    weights = (
        y_factor.astype(jnp.float32)[:, None, :] * t_factor.astype(jnp.float32)[None, :, :]
    ).reshape(cols_y * cols_t, -1)
    gram_z = jnp.dot(whole_z.T, whole_z, preferred_element_type=jnp.float32)
    local_y = jnp.dot(y_factor.T, y_factor, preferred_element_type=jnp.float32)
    local_t = jnp.dot(t_factor.T, t_factor, preferred_element_type=jnp.float32)
    gram_y = lax.psum(local_y, "yz")
    gram_t = lax.psum(local_t, "ta")
    own_rows = rows_x // (lax.axis_size("yz") * lax.axis_size("ta"))
    contracted = jnp.dot(
        snapshot.reshape(lax.axis_size(("yz", "ta")) * own_rows * cols_y * cols_t, cells_z),
        whole_z,
        preferred_element_type=jnp.float32,
    )
    contracted = contracted.reshape(lax.axis_size(("yz", "ta")) * own_rows, cols_y * cols_t, -1)
    summed = lax.psum_scatter(
        jnp.sum(contracted * weights[None], axis=1), ("yz", "ta"), scatter_dimension=0, tiled=True
    )
    normal_matrix = gram_y * gram_z * gram_t
    lower = jnp.linalg.cholesky(normal_matrix)
    return jax.scipy.linalg.cho_solve((lower, True), summed.T).T


def solution(mesh):
    return jax.shard_map(
        per_device,
        mesh=mesh,
        in_specs=(P("gx", "yz", "ta", None), P("yz", None), P("yz", None), P("ta", None)),
        out_specs=P(("gx", "yz", "ta"), None),
        check_vma=False,
    )
```

profile of v0, /device:TPU:2, one launch (start us, length us, event | category | flops | bytes accessed | tf_op | source)
XLA Modules:
  0.0 1102.3 jit_solution(11691255091061065439)
XLA Ops:
  6.5 1.7 fusion.13
  8.3 1.7 fusion.14
  10.1 0.7 convert_element_type.6
  10.8 0.7 convert_element_type.7
  11.5 208.6 %all-gather = bf16[64,4,256]{2,1,0:T(4,128)(2,1)S(1)} all-gather(bf16[1,4,256]{2,1,0:T(4,128)(2,1)} %bitcast.52), channel_id=1, replica_groups=mesh['gx'=2,'yz'=64,'ta'=4] {'yz'}, dimensions={0}, use_global_device_ids=true | all-gather | bytes 133120 | tf_op jit(solution)/shard_map/all_gather | solution.py:8
  220.1 5.6 copy.18
  225.7 4.5 multiply_reduce_fusion
  230.3 1.4 dynamic-slice.3
  232.4 571.4 %all-reduce.6.cloned.1.call-done = f32[256,256]{0,1:T(8,128)} async-done(((f32[256,256]{0,1:T(8,128)}), f32[256,256]{0,1:T(8,128)}) %all-reduce.6.cloned.1.call-update) | async-done | bytes 262160 | tf_op jit(solution)/shard_map/psum | solution.py:16
  803.8 52.3 %all-reduce.8.cloned.1.call-done = f32[256,256]{0,1:T(8,128)} async-done(((f32[256,256]{0,1:T(8,128)}), f32[256,256]{0,1:T(8,128)}) %all-reduce.8.cloned.1.call-update) | async-done | bytes 262160 | tf_op jit(solution)/shard_map/psum | solution.py:17
  856.1 1.3 fusion
  857.5 11.7 %cholesky.50 = f32[128,128]{1,0:T(8,128)S(1)} custom-call(f32[128,128]{1,0:T(8,128)S(1)} %cholesky.118), custom_call_target="Cholesky" | custom-call | tf_op jit(solution)/shard_map/jit(cholesky)/cholesky | solution.py:29
  869.3 9.8 custom-call.18
  879.6 11.9 %cholesky.105 = f32[128,128]{1,0:T(8,128)S(1)} custom-call(f32[128,128]{1,0:T(8,128)S(1)} %convolution_subtract_fusion), custom_call_target="Cholesky" | custom-call | tf_op jit(solution)/shard_map/jit(cholesky)/cholesky | solution.py:29
  891.5 0.7 compare_reduce_fusion
  893.6 4.1 while.1
  893.6 0.7 fusion.31
  894.3 1.3 bitcast_dynamic-update-slice_fusion.2
  895.7 0.7 fusion.31
  896.3 1.3 bitcast_dynamic-update-slice_fusion.2
  897.7 19.7 %custom-call.19 = f32[2,128,128]{1,2,0:T(8,128)S(1)} custom-call(f32[2,128,128]{2,1,0:T(8,128)S(1)} %get-tuple-element.12), custom_call_target="InvertDiagBlocksLowerTriangular" | custom-call | tf_op jit(solution)/shard_map/jit(_cho_solve)/triangular_solve | solution.py:30
  917.4 175.7 %all-reduce.10.cloned.1.call-done = f32[512,256]{1,0:T(8,128)} async-done(((f32[512,256]{1,0:T(8,128)}), f32[512,256]{1,0:T(8,128)}) %all-reduce.10.cloned.1.call-update) | async-done | bytes 524304
  1093.1 0.7 dynamic-slice_bitcast_fusion
  1095.1 0.6 maximum_bitcast_fusion
  (30 shorter events, 2.4 us)
Async XLA Ops:
  6.5 797.2 %all-reduce.6.cloned.1.call-start = ((), (), s32[]{:S(2)}) async-start(), calls=%async_computation | async-start | bytes 524288 | tf_op jit(solution)/shard_map/psum | solution.py:16
  8.3 847.8 %all-reduce.8.cloned.1.call-start = ((), (), s32[]{:S(2)}) async-start(), calls=%async_computation.1 | async-start | bytes 524288 | tf_op jit(solution)/shard_map/psum | solution.py:17
  10.0 1083.1 %all-reduce.10.cloned.1.call-start = ((), (), s32[]{:S(2)}) async-start(), calls=%async_computation.2 | async-start | bytes 1048576
Sparse Core Ops, SparseCore 0:
  10.3 793.4 all-reduce.5
  807.0 49.0 all-reduce.7
  861.1 231.9 all-reduce.9
where the time goes:
time: 1100 us
  waiting for transfers between devices  799 us (73%)
  blocking collectives  209 us (19%)
  other arithmetic  55.9 us (5%)
  between operations  15.2 us (1%)
  local copies, waits for them, and re-layouts  12 us (1%)
    psum x1, waiting for transfers between devices, per_device(): gram_y = lax.psum(local_y, 'yz')  571 us
    all_gather x1, blocking collectives, per_device(): whole_z = lax.all_gather(z_factor, 'yz', axis=0, tiled=True)  209 us
    unnamed x4, waiting for transfers between devices  176 us
    psum x1, waiting for transfers between devices, per_device(): gram_t = lax.psum(local_t, 'ta')  52.3 us
    another operation x6, other arithmetic, per_device(): lower = jnp.linalg.cholesky(normal_matrix)  34.2 us
  transfers between devices with their start and end apart: 3, of which 3 were waited for; matrix products, arithmetic and copies ran while one was open for 7% of the time, Pallas kernels for 0%

commit v1 on v0

v1 whole, which is shorter than its diff:
```python
import jax
import jax.numpy as jnp
from jax import lax
from jax.experimental import pallas as pl
from jax.experimental.pallas import tpu as pltpu
from jax.sharding import PartitionSpec as P

SUB = 8
SUPER = 32
TILE = 128
CONTRACT_LAST = (((1,), (0,)), ((), ()))
CONTRACT_ROWS = (((0,), (0,)), ((), ()))


def three_parts(values):
    high = values.astype(jnp.bfloat16)
    rest = values - high.astype(jnp.float32)
    middle = rest.astype(jnp.bfloat16)
    low = (rest - middle.astype(jnp.float32)).astype(jnp.bfloat16)
    return high, middle, low


def product_over_rows(left, right):
    left_high, left_middle, left_low = three_parts(left)
    right_high, right_middle, right_low = three_parts(right)
    lefts = jnp.concatenate([left_high, left_high, left_middle, left_high, left_low, left_middle], axis=0)
    rights = jnp.concatenate([right_high, right_middle, right_high, right_low, right_high, right_middle], axis=0)
    return lax.dot_general(lefts, rights, CONTRACT_ROWS, preferred_element_type=jnp.float32)


def inverse_cholesky_factor(matrix):
    rank = matrix.shape[0]
    lane = lax.broadcasted_iota(jnp.int32, (SUB, rank), 1)
    row = lax.broadcasted_iota(jnp.int32, (SUB, rank), 0)
    narrow_row = lax.broadcasted_iota(jnp.int32, (SUB, 128), 0)
    wide_lane = lax.broadcasted_iota(jnp.int32, (SUPER, rank), 1)
    wide_row = lax.broadcasted_iota(jnp.int32, (SUPER, rank), 0)
    wide = rank // 128
    rows = [matrix[start : start + SUB, :] for start in range(0, rank, SUB)]
    blocks = SUPER // SUB
    for first in range(0, rank, SUPER):
        panel = rows[first // SUB : first // SUB + blocks]
        for block in range(blocks):
            start = first + block * SUB
            below = range(block, blocks)
            column = {
                (j, i): jnp.broadcast_to(panel[i][:, start + j : start + j + 1], (SUB, 128))
                for j in range(SUB)
                for i in below
            }
            own = (lane >= start) & (lane < start + SUB)
            for i in below:
                identity = jnp.where(lane - start == row, 1.0, 0.0) if i == block else 0.0
                panel[i] = jnp.where(own, identity, panel[i])
            scale = None
            for j in range(SUB):
                pivot = jnp.broadcast_to(column[j, block][j : j + 1, :], (SUB, 128))
                root = lax.rsqrt(pivot)
                inverse = 1.0 / pivot
                scale = root if scale is None else jnp.where(narrow_row == j, root, scale)
                factor = {i: column[j, i] * inverse for i in below}
                if j == SUB - 1:
                    factor.pop(block)
                else:
                    factor[block] = jnp.where(narrow_row > j, factor[block], 0.0)
                for other in range(j + 1, SUB):
                    entry = jnp.broadcast_to(column[other, block][j : j + 1, :], (SUB, 128))
                    for i in factor:
                        column[other, i] = column[other, i] - factor[i] * entry
                entry = jnp.broadcast_to(panel[block][j : j + 1, :], (SUB, rank))
                for i in factor:
                    panel[i] = panel[i] - jnp.concatenate([factor[i]] * wide, axis=1) * entry
            panel[block] = panel[block] * jnp.concatenate([scale] * wide, axis=1)
        rows[first // SUB : first // SUB + blocks] = panel
        end = first + SUPER
        if end < rank:
            upper = jnp.concatenate(panel, axis=0)
            done = jnp.where((wide_lane < end) & (wide_lane - first > wide_row), 0.0, upper)
            from_lane = end // 128 * 128
            update = product_over_rows(upper[:, from_lane:], done)
            fresh = (lane >= first) & (lane < end)
            for i in range(end // SUB, rank // SUB):
                at = i * SUB - from_lane
                rows[i] = jnp.where(fresh, 0.0, rows[i]) - update[at : at + SUB, :]
    kept = [jnp.where(lane <= row + i * SUB, rows[i], 0.0) for i in range(rank // SUB)]
    return jnp.concatenate(kept, axis=0)


def inverse_kernel(y_ref, other_y_ref, z_ref, t_ref, high_ref, middle_ref, low_ref):
    def gram(factor):
        return lax.dot_general(factor, factor, CONTRACT_ROWS, preferred_element_type=jnp.float32)

    gram_y = gram(y_ref[...]) + gram(other_y_ref[...])
    normal_matrix = gram_y * gram(z_ref[...]) * gram(t_ref[...])
    inverse_factor = inverse_cholesky_factor(normal_matrix)
    inverse = product_over_rows(inverse_factor, inverse_factor)
    high_ref[...], middle_ref[...], low_ref[...] = three_parts(inverse)


def contract_kernel(snapshot_ref, z_ref, y_ref, t_ref, out_ref):
    z, y, t = z_ref[...], y_ref[...], t_ref[...]
    cols_y, cols_t = y.shape[0], t.shape[0]
    group = out_ref.shape[1]
    for start in range(0, snapshot_ref.shape[1], TILE):
        total = None
        for j in range(cols_y):
            for l in range(cols_t):
                part = lax.dot_general(
                    snapshot_ref[j * cols_t + l, start : start + TILE, :],
                    z,
                    CONTRACT_LAST,
                    preferred_element_type=jnp.float32,
                )
                part = part * (y[j : j + 1, :] * t[l : l + 1, :])
                total = part if total is None else total + part
        out_ref[start // group : (start + TILE) // group] = total.reshape(TILE // group, group, total.shape[1])


def finish_kernel(parts_ref, high_ref, middle_ref, low_ref, out_ref):
    summed = jnp.sum(parts_ref[...], axis=0)
    count = summed.shape[0]
    lefts = jnp.concatenate([part.astype(jnp.float32) for part in three_parts(summed)], axis=0).astype(jnp.bfloat16)

    def product(right_ref):
        return lax.dot_general(lefts, right_ref[...], CONTRACT_LAST, preferred_element_type=jnp.float32)

    by_high, by_middle, by_low = product(high_ref), product(middle_ref), product(low_ref)
    small = by_low[:count] + by_middle[count : 2 * count] + by_high[2 * count :]
    out_ref[...] = by_high[:count] + (by_middle[:count] + by_high[count : 2 * count] + small)


def copies_kernel(z_ref, y_ref, out_ref):
    z, y = z_ref[...].astype(jnp.float32), y_ref[...].astype(jnp.float32)
    half = y.shape[0] // 2
    own_half = jnp.where(lax.axis_index("gx") == 0, y[:half], y[half:])
    rows = jnp.concatenate([z, own_half], axis=0).astype(jnp.bfloat16)
    out_ref[...] = jnp.broadcast_to(rows[None], out_ref.shape)


def kernel_call(body, out_shape, flops, bytes_accessed, vmem_mib=24):
    return pl.pallas_call(
        body,
        out_shape=out_shape,
        compiler_params=pltpu.CompilerParams(vmem_limit_bytes=vmem_mib << 20),
        cost_estimate=pl.CostEstimate(flops=flops, bytes_accessed=bytes_accessed, transcendentals=0),
    )


def gathered(y_factor, z_factor):
    steps, blocks = lax.axis_size("ta"), lax.axis_size("yz")
    rows_z, rank = z_factor.shape
    half = y_factor.shape[0] // 2
    groups = [[b * steps + (g + b % 2 * (steps // 2)) % steps for b in range(blocks)] for g in range(steps)]
    shape = jax.ShapeDtypeStruct((blocks, rows_z + half, rank), z_factor.dtype)
    copies = kernel_call(copies_kernel, shape, 0, 2 * shape.size, 60)(z_factor, y_factor)
    arrived = lax.all_to_all(copies, ("yz", "ta"), 0, 0, axis_index_groups=groups)
    return arrived[:, :rows_z].reshape(blocks * rows_z, rank), arrived[:, rows_z:].reshape(blocks * half, rank)


def per_device(snapshot, y_factor, z_factor, t_factor):
    rows_x, cols_y, cols_t, cells_z = snapshot.shape
    rank = z_factor.shape[1]
    devices = lax.axis_size(("yz", "ta"))
    own_rows = rows_x // devices
    steps = lax.axis_size("ta")

    def swapped(array, distance):
        return lax.ppermute(array, "ta", [(i, i ^ distance) for i in range(steps)])

    whole_z, half_y = gathered(y_factor, z_factor)
    t_wide = t_factor.astype(jnp.float32)
    t_pair = swapped(t_wide, 1)
    whole_z, t_pair = lax.optimization_barrier((whole_z, t_pair))
    t_pair = jnp.concatenate([t_wide, t_pair], axis=0)
    ordered = snapshot.transpose(1, 2, 0, 3).reshape(cols_y * cols_t, rows_x, cells_z)
    own_sums = jax.ShapeDtypeStruct((devices, own_rows, rank), jnp.float32)
    sums = kernel_call(contract_kernel, own_sums, 2 * snapshot.size * rank, 2 * snapshot.size)(
        ordered, whole_z, y_factor.astype(jnp.float32), t_wide
    )
    parts = lax.all_to_all(sums, ("yz", "ta"), 0, 0)
    other_y = lax.ppermute(half_y, "gx", [(0, 1), (1, 0)])
    whole_t = jnp.concatenate([t_pair, swapped(t_pair, 2)], axis=0)
    whole_t = jnp.concatenate([whole_t, jnp.zeros_like(whole_t)], axis=0).astype(jnp.bfloat16)
    square = jax.ShapeDtypeStruct((rank, rank), jnp.bfloat16)
    inverse = kernel_call(inverse_kernel, [square] * 3, 100_000_000, 1_000_000)(half_y, other_y, whole_z, whole_t)
    own = jax.ShapeDtypeStruct((own_rows, rank), jnp.float32)
    return kernel_call(finish_kernel, own, 6 * rank * rank, 4 * rows_x * rank)(parts, *inverse)


def solution(mesh):
    return jax.shard_map(
        per_device,
        mesh=mesh,
        in_specs=(P("gx", "yz", "ta", None), P("yz", None), P("yz", None), P("ta", None)),
        out_specs=P(("gx", "yz", "ta"), None),
        check_vma=False,
    )
```

time: 1100 us -> 72.3 us (0.07)
  the two profiles are of different devices: /device:TPU:2 before, /device:TPU:64 now
where the time goes in v1:
time: 72.3 us; the launch traced here: 71.8 us
  starting transfers between devices  40.2 us (56%)
  Pallas kernels  13.1 us (18%)
  waiting for transfers between devices  8.87 us (12%)
  local copies, waits for them, and re-layouts  8.07 us (11%)
  other arithmetic  1.46 us (2%)
    all_to_all x1, starting transfers between devices, gathered(): lax.all_to_all(copies, ('yz', 'ta'), 0, 0, axis_index_groups=groups)  16.7 us
    all_to_all x1, starting transfers between devices, per_device(): parts = lax.all_to_all(sums, ('yz', 'ta'), 0, 0)  14.6 us
    pallas_call x1, Pallas kernels, per_device(): kernel_call(inverse_kernel, [square] * 3, 100000000, 1000000)  8.56 us
    ppermute x2, starting transfers between devices, swapped(): return lax.ppermute(array, 'ta', [(i, i ^ distance) for i in range(steps)])  6.86 us
    transpose x1, local copies, waits for them, and re-layouts, per_device(): snapshot.transpose(1, 2, 0, 3).reshape(cols_y * cols_t, rows_x, cells_z)  5.64 us
    ppermute x2, waiting for transfers between devices, swapped(): return lax.ppermute(array, 'ta', [(i, i ^ distance) for i in range(steps)])  3.74 us
    all_to_all x1, waiting for transfers between devices, gathered(): lax.all_to_all(copies, ('yz', 'ta'), 0, 0, axis_index_groups=groups)  2.62 us
    all_to_all x1, waiting for transfers between devices, per_device(): parts = lax.all_to_all(sums, ('yz', 'ta'), 0, 0)  2.51 us
  transfers between devices with their start and end apart: 5, of which 3 were waited for; matrix products, arithmetic and copies ran while one was open for 10% of the time, Pallas kernels for 12%

profile of v1, /device:TPU:64, one launch (start us, length us, event | category | flops | bytes accessed | tf_op | source)
XLA Modules:
  0.0 71.8 jit_solution(14332392561738997864)
XLA Ops:
  0.0 1.4 %shard_map.46 = bf16[64,8,256]{2,1,0:T(8,128)(2,1)} custom-call(bf16[4,256]{1,0:T(4,128)(2,1)} %z_ref.1, bf16[8,256]{1,0:T(8,128)(2,1)} %y_ref.1), custom_call_target="tpu_custom_call" | custom-call | bytes 262144 | tf_op jit(solution)/shard_map/pallas_call | solution.py:155
  1.4 16.7 %all-to-all-start = ((bf16[64,8,256]{2,1,0:T(8,128)(2,1)}), bf16[64,8,256]{2,1,0:T(8,128)(2,1)S(1)}, u32[]{:S(2)}, u32[]{:S(2)}) async-start(bf16[64,8,256]{2,1,0:T(8,128)(2,1)} %shard_map.46), calls=%async_computation | async-start | bytes 524288 | tf_op jit(solution)/shard_map/all_to_all | solution.py:156
  18.1 2.6 %collective-permute-start = (bf16[2,256]{1,0:T(2,128)(2,1)}, bf16[2,256]{1,0:T(2,128)(2,1)S(1)}, u32[]{:S(2)}, u32[]{:S(2)}) collective-permute-start(bf16[2,256]{1,0:T(2,128)(2,1)} %param.7), channel_id=1, source_target_pairs={{0,1},{1,0},{2,3},{3,2},{4,5},{5,4},{6,7},{7,6},{8,9},{9,8},{10,11... | collective-permute-start | bytes 3080 | tf_op jit(solution)/shard_map/ppermute | solution.py:168
  20.7 0.7 convert_element_type.8.y_ref
  21.4 0.7 convert_element_type.7.t_ref
  22.1 5.6 %copy.5 = bf16[8,2,512,256]{3,2,1,0:T(8,128)(2,1)} copy(bf16[8,2,512,256]{3,1,0,2:T(2,128)(2,1)} %bitcast.3) | data formatting | bytes 8388608 | tf_op jit(solution)/shard_map/transpose | solution.py:175
  27.7 0.0 copy-start.1
  27.7 2.6 %all-to-all-done = bf16[64,8,256]{2,1,0:T(8,128)(2,1)S(1)} async-done(((bf16[64,8,256]{2,1,0:T(8,128)(2,1)}), bf16[64,8,256]{2,1,0:T(8,128)(2,1)S(1)}, u32[]{:S(2)}, u32[]{:S(2)}) %all-to-all-start) | async-done | bytes 262176 | tf_op jit(solution)/shard_map/all_to_all | solution.py:156
  30.3 0.1 fusion
  30.5 0.0 collective-permute-done
  30.5 0.0 copy-start
  30.5 2.2 %copy-done = bf16[8,2,512,256]{3,2,1,0:T(8,128)(2,1)S(1)} copy-done((bf16[8,2,512,256]{3,2,1,0:T(8,128)(2,1)S(1)}, bf16[8,2,512,256]{3,2,1,0:T(8,128)(2,1)}, u32[]{:S(2)}) %copy-start) | copy-done | bytes 4194328
  32.7 2.1 %shard_map.47 = f32[256,2,256]{2,1,0:T(2,128)} custom-call(bf16[16,512,256]{2,1,0:T(8,128)(2,1)S(1)} %bitcast.2, bf16[256,256]{1,0:T(8,128)(2,1)S(1)} %reshape.10.z_ref, f32[8,256]{1,0:T(8,128)S(1)} %convert_element_type.8.y_ref, f32[2,256]{1,0:T(2,128)S(1)} %convert_element_type.7.t_ref), custom_call_target="tpu_custom_call" | custom-call | flops 1073741824 | bytes 4194304 | tf_op jit(solution)/shard_map/pallas_call | solution.py:177
  34.8 14.6 %all-to-all-start.1 = ((f32[256,2,256]{2,1,0:T(2,128)}), f32[256,2,256]{2,1,0:T(2,128)S(1)}, u32[]{:S(2)}, u32[]{:S(2)}) async-start(f32[256,2,256]{2,1,0:T(2,128)} %shard_map.47), calls=%async_computation.1 | async-start | bytes 1048576 | tf_op jit(solution)/shard_map/all_to_all | solution.py:180
  49.4 4.3 %collective-permute-start.2 = (bf16[4,256]{1,0:T(4,128)(2,1)S(1)}, bf16[4,256]{1,0:T(4,128)(2,1)S(1)}, u32[]{:S(2)}, u32[]{:S(2)}) collective-permute-start(bf16[4,256]{1,0:T(4,128)(2,1)S(1)} %pad_maximum_fusion), channel_id=1, source_target_pairs={{0,2},{1,3},{2,0},{3,1},{4,6},{5,7},{6,4},{7,5},{8,10},{9,11},{10,... | collective-permute-start | bytes 6152 | tf_op jit(solution)/shard_map/ppermute | solution.py:168
  53.7 0.1 pad.3.clone
  53.8 2.1 %collective-permute-start.1 = (bf16[256,256]{1,0:T(8,128)(2,1)S(1)}, bf16[256,256]{1,0:T(8,128)(2,1)S(1)}, u32[]{:S(2)}, u32[]{:S(2)}) collective-permute-start(bf16[256,256]{1,0:T(8,128)(2,1)S(1)} %reshape.11.y_ref), channel_id=1, source_target_pairs={{0,256},{256,0},{1,257},{257,1},{2,258},{258,2},{3,259},{259,3},{4... | collective-permute-start | bytes 393224 | tf_op jit(solution)/shard_map/ppermute | solution.py:181
  55.9 3.7 %collective-permute-done.2 = bf16[4,256]{1,0:T(4,128)(2,1)S(1)} collective-permute-done((bf16[4,256]{1,0:T(4,128)(2,1)S(1)}, bf16[4,256]{1,0:T(4,128)(2,1)S(1)}, u32[]{:S(2)}, u32[]{:S(2)}) %collective-permute-start.2) | collective-permute-done | bytes 2080 | tf_op jit(solution)/shard_map/ppermute | solution.py:168
  59.6 0.0 copy-done.1
  59.6 0.1 maximum_maximum_fusion.t_ref
  59.7 0.0 collective-permute-done.1.other_y_ref
  59.7 8.6 %shard_map.48 = (bf16[256,256]{1,0:T(8,128)(2,1)S(1)}, bf16[256,256]{1,0:T(8,128)(2,1)S(1)}, bf16[256,256]{1,0:T(8,128)(2,1)S(1)}) custom-call(bf16[256,256]{1,0:T(8,128)(2,1)S(1)} %reshape.11.y_ref, bf16[256,256]{1,0:T(8,128)(2,1)S(1)} %collective-permute-done.1.other_y_ref, bf16[256,256]{1,0:T(8,128)(2,1)S(1)} %reshape.10.z_ref, ...), custom_call_target="tpu_custom_call" | custom-call | flops 100000000 | bytes 1000000 | tf_op jit(solution)/shard_map/pallas_call | solution.py:185
  68.3 2.5 %all-to-all-done.1.parts_ref = f32[256,2,256]{2,1,0:T(2,128)S(1)} async-done(((f32[256,2,256]{2,1,0:T(2,128)}), f32[256,2,256]{2,1,0:T(2,128)S(1)}, u32[]{:S(2)}, u32[]{:S(2)}) %all-to-all-start.1) | async-done | bytes 524320 | tf_op jit(solution)/shard_map/all_to_all | solution.py:180
  70.8 1.0 %shard_map.49 = f32[2,256]{1,0:T(2,128)} custom-call(f32[256,2,256]{2,1,0:T(2,128)S(1)} %all-to-all-done.1.parts_ref, bf16[256,256]{1,0:T(8,128)(2,1)S(1)} %get-tuple-element.12.high_ref, bf16[256,256]{1,0:T(8,128)(2,1)S(1)} %get-tuple-element.13.middle_ref, bf16[256,256]{1,0:T(8,128)(2,1)S(1)} %get-tuple-element.14.low_ref), custom_call_target="tpu_custom_call" | custom-call | flops 393216 | bytes 524288 | tf_op jit(solution)/shard_map/pallas_call | solution.py:187
  (4 shorter events, 0.1 us)
Async XLA Ops:
  1.4 28.9 %all-to-all-start = ((bf16[64,8,256]{2,1,0:T(8,128)(2,1)}), bf16[64,8,256]{2,1,0:T(8,128)(2,1)S(1)}, u32[]{:S(2)}, u32[]{:S(2)}) async-start(bf16[64,8,256]{2,1,0:T(8,128)(2,1)} %shard_map.46), calls=%async_computation | async-start | bytes 524288 | tf_op jit(solution)/shard_map/all_to_all | solution.py:156
  18.1 12.4 %collective-permute-start = (bf16[2,256]{1,0:T(2,128)(2,1)}, bf16[2,256]{1,0:T(2,128)(2,1)S(1)}, u32[]{:S(2)}, u32[]{:S(2)}) collective-permute-start(bf16[2,256]{1,0:T(2,128)(2,1)} %param.7), channel_id=1, source_target_pairs={{0,1},{1,0},{2,3},{3,2},{4,5},{5,4},{6,7},{7,6},{8,9},{9,8},{10,11... | collective-permute-start | bytes 3080 | tf_op jit(solution)/shard_map/ppermute | solution.py:168
  27.7 31.9 %copy-start.1 = (bf16[2,256]{1,0:T(2,128)(2,1)S(1)}, bf16[2,256]{1,0:T(2,128)(2,1)}, u32[]{:S(2)}) copy-start(bf16[2,256]{1,0:T(2,128)(2,1)} %param.7) | copy-start | bytes 3076
  30.5 2.2 %copy-start = (bf16[8,2,512,256]{3,2,1,0:T(8,128)(2,1)S(1)}, bf16[8,2,512,256]{3,2,1,0:T(8,128)(2,1)}, u32[]{:S(2)}) copy-start(bf16[8,2,512,256]{3,2,1,0:T(8,128)(2,1)} %copy.5) | copy-start | bytes 12582916
  34.8 36.0 %all-to-all-start.1 = ((f32[256,2,256]{2,1,0:T(2,128)}), f32[256,2,256]{2,1,0:T(2,128)S(1)}, u32[]{:S(2)}, u32[]{:S(2)}) async-start(f32[256,2,256]{2,1,0:T(2,128)} %shard_map.47), calls=%async_computation.1 | async-start | bytes 1048576 | tf_op jit(solution)/shard_map/all_to_all | solution.py:180
  49.4 10.2 %collective-permute-start.2 = (bf16[4,256]{1,0:T(4,128)(2,1)S(1)}, bf16[4,256]{1,0:T(4,128)(2,1)S(1)}, u32[]{:S(2)}, u32[]{:S(2)}) collective-permute-start(bf16[4,256]{1,0:T(4,128)(2,1)S(1)} %pad_maximum_fusion), channel_id=1, source_target_pairs={{0,2},{1,3},{2,0},{3,1},{4,6},{5,7},{6,4},{7,5},{8,10},{9,11},{10,... | collective-permute-start | bytes 6152 | tf_op jit(solution)/shard_map/ppermute | solution.py:168
  53.8 5.9 %collective-permute-start.1 = (bf16[256,256]{1,0:T(8,128)(2,1)S(1)}, bf16[256,256]{1,0:T(8,128)(2,1)S(1)}, u32[]{:S(2)}, u32[]{:S(2)}) collective-permute-start(bf16[256,256]{1,0:T(8,128)(2,1)S(1)} %reshape.11.y_ref), channel_id=1, source_target_pairs={{0,256},{256,0},{1,257},{257,1},{2,258},{258,2},{3,259},{259,3},{4... | collective-permute-start | bytes 393224 | tf_op jit(solution)/shard_map/ppermute | solution.py:181

commit v2 on v1

--- a/solution.py
+++ b/solution.py
@@ -97,16 +97,23 @@
     high_ref[...], middle_ref[...], low_ref[...] = three_parts(inverse)
 
 
-def contract_kernel(snapshot_ref, z_ref, y_ref, t_ref, out_ref):
-    z, y, t = z_ref[...], y_ref[...], t_ref[...]
+def contract_kernel(snapshot_ref, z_ref, y_ref, t_ref, out_ref, held, arrived):
+    rows_x = snapshot_ref.shape[1]
+    copies = []
+    for index, start in enumerate(range(0, rows_x, TILE)):
+        rows = pl.ds(start, TILE)
+        copies.append(pltpu.make_async_copy(snapshot_ref.at[:, rows], held.at[:, rows], arrived.at[index]))
+        copies[-1].start()
+    z, y, t = z_ref[...], y_ref[...].astype(jnp.float32), t_ref[...].astype(jnp.float32)
     cols_y, cols_t = y.shape[0], t.shape[0]
     group = out_ref.shape[1]
-    for start in range(0, snapshot_ref.shape[1], TILE):
+    for copy, start in zip(copies, range(0, rows_x, TILE)):
+        copy.wait()
         total = None
         for j in range(cols_y):
             for l in range(cols_t):
                 part = lax.dot_general(
-                    snapshot_ref[j * cols_t + l, start : start + TILE, :],
+                    held[j * cols_t + l, start : start + TILE, :],
                     z,
                     CONTRACT_LAST,
                     preferred_element_type=jnp.float32,
@@ -173,10 +180,21 @@
     whole_z, t_pair = lax.optimization_barrier((whole_z, t_pair))
     t_pair = jnp.concatenate([t_wide, t_pair], axis=0)
     ordered = snapshot.transpose(1, 2, 0, 3).reshape(cols_y * cols_t, rows_x, cells_z)
-    own_sums = jax.ShapeDtypeStruct((devices, own_rows, rank), jnp.float32)
-    sums = kernel_call(contract_kernel, own_sums, 2 * snapshot.size * rank, 2 * snapshot.size)(
-        ordered, whole_z, y_factor.astype(jnp.float32), t_wide
-    )
+    in_vmem = pl.BlockSpec(memory_space=pltpu.VMEM)
+    sums = pl.pallas_call(
+        contract_kernel,
+        in_specs=[pl.BlockSpec(memory_space=pltpu.HBM), in_vmem, in_vmem, in_vmem],
+        out_specs=in_vmem,
+        out_shape=jax.ShapeDtypeStruct((devices, own_rows, rank), jnp.float32),
+        scratch_shapes=[
+            pltpu.VMEM(ordered.shape, ordered.dtype),
+            pltpu.SemaphoreType.DMA((rows_x // TILE,)),
+        ],
+        compiler_params=pltpu.CompilerParams(vmem_limit_bytes=52 << 20),
+        cost_estimate=pl.CostEstimate(
+            flops=2 * snapshot.size * rank, bytes_accessed=2 * snapshot.size, transcendentals=0
+        ),
+    )(ordered, whole_z, y_factor, t_factor)
     parts = lax.all_to_all(sums, ("yz", "ta"), 0, 0)
     other_y = lax.ppermute(half_y, "gx", [(0, 1), (1, 0)])
     whole_t = jnp.concatenate([t_pair, swapped(t_pair, 2)], axis=0)

time: 72.3 us -> 70.5 us (0.975)
  local copies, waits for them, and re-layouts: 8.07 us -> 5.91 us
  Pallas kernels: 13.1 us -> 14.9 us
  other arithmetic: 1.46 us -> 0.08 us
  waiting for transfers between devices: 8.87 us -> 10.2 us
  starting transfers between devices: 40.2 us -> 38.9 us
    unnamed x4, local copies, waits for them, and re-layouts: 2.18 us -> 0.01 us
    pallas_call x1, Pallas kernels: 2.08 us -> 3.88 us  [per_device(): pl.pallas_call(contract_kernel, in_specs=[pl.BlockSpec(memory_space=pltpu...]
    convert_element_type x2 -> x0, other arithmetic: 1.37 us -> none  [the longest x1 0.69 us: per_device(): y_factor.astype(jnp.float32)]
    all_to_all x1, starting transfers between devices: 14.6 us -> 13.2 us  [per_device(): parts = lax.all_to_all(sums, ('yz', 'ta'), 0, 0)]
    all_to_all x1, waiting for transfers between devices: 2.62 us -> 3.96 us  [gathered(): lax.all_to_all(copies, ('yz', 'ta'), 0, 0, axis_index_groups=groups)]
  transfers between devices with their start and end apart: 5 -> 5, of which waited for: 3 -> 3; matrix products, arithmetic and copies ran while one was open for 10% -> 9% of each run, Pallas kernels for 12% -> 12%
where the time goes in v2:
time: 70.5 us; the launch traced here: 70.1 us
  starting transfers between devices  38.9 us (55%)
  Pallas kernels  14.9 us (21%)
  waiting for transfers between devices  10.2 us (14%)
  local copies, waits for them, and re-layouts  5.91 us (8%)
    all_to_all x1, starting transfers between devices, gathered(): lax.all_to_all(copies, ('yz', 'ta'), 0, 0, axis_index_groups=groups)  16.7 us
    all_to_all x1, starting transfers between devices, per_device(): parts = lax.all_to_all(sums, ('yz', 'ta'), 0, 0)  13.2 us
    pallas_call x1, Pallas kernels, per_device(): kernel_call(inverse_kernel, [square] * 3, 100000000, 1000000)  8.56 us
    ppermute x2, starting transfers between devices, swapped(): return lax.ppermute(array, 'ta', [(i, i ^ distance) for i in range(steps)])  6.86 us
    transpose x1, local copies, waits for them, and re-layouts, per_device(): snapshot.transpose(1, 2, 0, 3).reshape(cols_y * cols_t, rows_x, cells_z)  5.65 us
    all_to_all x1, waiting for transfers between devices, gathered(): lax.all_to_all(copies, ('yz', 'ta'), 0, 0, axis_index_groups=groups)  3.96 us
    pallas_call x1, Pallas kernels, per_device(): pl.pallas_call(contract_kernel, in_specs=[pl.BlockSpec(memory_space=pltpu...  3.88 us
    ppermute x2, waiting for transfers between devices, swapped(): return lax.ppermute(array, 'ta', [(i, i ^ distance) for i in range(steps)])  3.75 us
  transfers between devices with their start and end apart: 5, of which 3 were waited for; matrix products, arithmetic and copies ran while one was open for 9% of the time, Pallas kernels for 12%

profile of v2, /device:TPU:64, one launch (start us, length us, event | category | flops | bytes accessed | tf_op | source)
XLA Modules:
  0.0 70.1 jit_solution(6080931180719313102)
XLA Ops:
  0.0 1.4 %shard_map.46 = bf16[64,8,256]{2,1,0:T(8,128)(2,1)} custom-call(bf16[4,256]{1,0:T(4,128)(2,1)} %z_ref.1, bf16[8,256]{1,0:T(8,128)(2,1)} %y_ref.3), custom_call_target="tpu_custom_call" | custom-call | bytes 262144 | tf_op jit(solution)/shard_map/pallas_call | solution.py:162
  1.4 16.7 %all-to-all-start = ((bf16[64,8,256]{2,1,0:T(8,128)(2,1)}), bf16[64,8,256]{2,1,0:T(8,128)(2,1)S(1)}, u32[]{:S(2)}, u32[]{:S(2)}) async-start(bf16[64,8,256]{2,1,0:T(8,128)(2,1)} %shard_map.46), calls=%async_computation | async-start | bytes 524288 | tf_op jit(solution)/shard_map/all_to_all | solution.py:163
  18.1 2.6 %collective-permute-start = (bf16[2,256]{1,0:T(2,128)(2,1)}, bf16[2,256]{1,0:T(2,128)(2,1)S(1)}, u32[]{:S(2)}, u32[]{:S(2)}) collective-permute-start(bf16[2,256]{1,0:T(2,128)(2,1)} %t_ref.1), channel_id=1, source_target_pairs={{0,1},{1,0},{2,3},{3,2},{4,5},{5,4},{6,7},{7,6},{8,9},{9,8},{10,11... | collective-permute-start | bytes 3080 | tf_op jit(solution)/shard_map/ppermute | solution.py:175
  20.7 0.0 copy-start
  20.7 0.0 copy-start.1
  20.7 5.7 %copy.5 = bf16[8,2,512,256]{3,2,1,0:T(8,128)(2,1)} copy(bf16[8,2,512,256]{3,1,0,2:T(2,128)(2,1)} %bitcast.3) | data formatting | bytes 8388608 | tf_op jit(solution)/shard_map/transpose | solution.py:182
  26.4 4.0 %all-to-all-done = bf16[64,8,256]{2,1,0:T(8,128)(2,1)S(1)} async-done(((bf16[64,8,256]{2,1,0:T(8,128)(2,1)}), bf16[64,8,256]{2,1,0:T(8,128)(2,1)S(1)}, u32[]{:S(2)}, u32[]{:S(2)}) %all-to-all-start) | async-done | bytes 262176 | tf_op jit(solution)/shard_map/all_to_all | solution.py:163
  30.3 0.1 fusion
  30.5 0.0 collective-permute-done
  30.5 0.0 copy-done
  30.5 0.0 copy-done.1
  30.5 3.9 %shard_map.47 = f32[256,2,256]{2,1,0:T(2,128)} custom-call(bf16[16,512,256]{2,1,0:T(8,128)(2,1)} %bitcast.2, bf16[256,256]{1,0:T(8,128)(2,1)S(1)} %reshape.10.z_ref, bf16[8,256]{1,0:T(8,128)(2,1)S(1)} %copy-done, bf16[2,256]{1,0:T(2,128)(2,1)S(1)} %copy-done.1), custom_call_target="tpu_custom_call" | custom-call | flops 1073741824 | bytes 4194304 | tf_op jit(solution)/shard_map/pallas_call | solution.py:184
  34.4 13.2 %all-to-all-start.1 = ((f32[256,2,256]{2,1,0:T(2,128)}), f32[256,2,256]{2,1,0:T(2,128)S(1)}, u32[]{:S(2)}, u32[]{:S(2)}) async-start(f32[256,2,256]{2,1,0:T(2,128)} %shard_map.47), calls=%async_computation.1 | async-start | bytes 1048576 | tf_op jit(solution)/shard_map/all_to_all | solution.py:198
  47.7 4.3 %collective-permute-start.2 = (bf16[4,256]{1,0:T(4,128)(2,1)S(1)}, bf16[4,256]{1,0:T(4,128)(2,1)S(1)}, u32[]{:S(2)}, u32[]{:S(2)}) collective-permute-start(bf16[4,256]{1,0:T(4,128)(2,1)S(1)} %pad_maximum_fusion), channel_id=1, source_target_pairs={{0,2},{1,3},{2,0},{3,1},{4,6},{5,7},{6,4},{7,5},{8,10},{9,11},{10,... | collective-permute-start | bytes 6152 | tf_op jit(solution)/shard_map/ppermute | solution.py:175
  52.0 0.1 pad.3.clone
  52.1 2.1 %collective-permute-start.1 = (bf16[256,256]{1,0:T(8,128)(2,1)S(1)}, bf16[256,256]{1,0:T(8,128)(2,1)S(1)}, u32[]{:S(2)}, u32[]{:S(2)}) collective-permute-start(bf16[256,256]{1,0:T(8,128)(2,1)S(1)} %reshape.11.y_ref), channel_id=1, source_target_pairs={{0,256},{256,0},{1,257},{257,1},{2,258},{258,2},{3,259},{259,3},{4... | collective-permute-start | bytes 393224 | tf_op jit(solution)/shard_map/ppermute | solution.py:199
  54.2 3.7 %collective-permute-done.2 = bf16[4,256]{1,0:T(4,128)(2,1)S(1)} collective-permute-done((bf16[4,256]{1,0:T(4,128)(2,1)S(1)}, bf16[4,256]{1,0:T(4,128)(2,1)S(1)}, u32[]{:S(2)}, u32[]{:S(2)}) %collective-permute-start.2) | collective-permute-done | bytes 2080 | tf_op jit(solution)/shard_map/ppermute | solution.py:175
  57.9 0.1 maximum_maximum_fusion.t_ref
  58.0 0.0 collective-permute-done.1.other_y_ref
  58.0 8.6 %shard_map.48 = (bf16[256,256]{1,0:T(8,128)(2,1)S(1)}, bf16[256,256]{1,0:T(8,128)(2,1)S(1)}, bf16[256,256]{1,0:T(8,128)(2,1)S(1)}) custom-call(bf16[256,256]{1,0:T(8,128)(2,1)S(1)} %reshape.11.y_ref, bf16[256,256]{1,0:T(8,128)(2,1)S(1)} %collective-permute-done.1.other_y_ref, bf16[256,256]{1,0:T(8,128)(2,1)S(1)} %reshape.10.z_ref, ...), custom_call_target="tpu_custom_call" | custom-call | flops 100000000 | bytes 1000000 | tf_op jit(solution)/shard_map/pallas_call | solution.py:203
  66.6 2.5 %all-to-all-done.1.parts_ref = f32[256,2,256]{2,1,0:T(2,128)S(1)} async-done(((f32[256,2,256]{2,1,0:T(2,128)}), f32[256,2,256]{2,1,0:T(2,128)S(1)}, u32[]{:S(2)}, u32[]{:S(2)}) %all-to-all-start.1) | async-done | bytes 524320 | tf_op jit(solution)/shard_map/all_to_all | solution.py:198
  69.1 1.0 %shard_map.49 = f32[2,256]{1,0:T(2,128)} custom-call(f32[256,2,256]{2,1,0:T(2,128)S(1)} %all-to-all-done.1.parts_ref, bf16[256,256]{1,0:T(8,128)(2,1)S(1)} %get-tuple-element.12.high_ref, bf16[256,256]{1,0:T(8,128)(2,1)S(1)} %get-tuple-element.13.middle_ref, bf16[256,256]{1,0:T(8,128)(2,1)S(1)} %get-tuple-element.14.low_ref), custom_call_target="tpu_custom_call" | custom-call | flops 393216 | bytes 524288 | tf_op jit(solution)/shard_map/pallas_call | solution.py:205
  (4 shorter events, 0.1 us)
Async XLA Ops:
  1.4 28.9 %all-to-all-start = ((bf16[64,8,256]{2,1,0:T(8,128)(2,1)}), bf16[64,8,256]{2,1,0:T(8,128)(2,1)S(1)}, u32[]{:S(2)}, u32[]{:S(2)}) async-start(bf16[64,8,256]{2,1,0:T(8,128)(2,1)} %shard_map.46), calls=%async_computation | async-start | bytes 524288 | tf_op jit(solution)/shard_map/all_to_all | solution.py:163
  18.1 12.4 %collective-permute-start = (bf16[2,256]{1,0:T(2,128)(2,1)}, bf16[2,256]{1,0:T(2,128)(2,1)S(1)}, u32[]{:S(2)}, u32[]{:S(2)}) collective-permute-start(bf16[2,256]{1,0:T(2,128)(2,1)} %t_ref.1), channel_id=1, source_target_pairs={{0,1},{1,0},{2,3},{3,2},{4,5},{5,4},{6,7},{7,6},{8,9},{9,8},{10,11... | collective-permute-start | bytes 3080 | tf_op jit(solution)/shard_map/ppermute | solution.py:175
  20.7 9.8 %copy-start = (bf16[8,256]{1,0:T(8,128)(2,1)S(1)}, bf16[8,256]{1,0:T(8,128)(2,1)}, u32[]{:S(2)}) copy-start(bf16[8,256]{1,0:T(8,128)(2,1)} %y_ref.3) | copy-start | bytes 12292
  20.7 9.8 %copy-start.1 = (bf16[2,256]{1,0:T(2,128)(2,1)S(1)}, bf16[2,256]{1,0:T(2,128)(2,1)}, u32[]{:S(2)}) copy-start(bf16[2,256]{1,0:T(2,128)(2,1)} %t_ref.1) | copy-start | bytes 3076
  34.4 34.7 %all-to-all-start.1 = ((f32[256,2,256]{2,1,0:T(2,128)}), f32[256,2,256]{2,1,0:T(2,128)S(1)}, u32[]{:S(2)}, u32[]{:S(2)}) async-start(f32[256,2,256]{2,1,0:T(2,128)} %shard_map.47), calls=%async_computation.1 | async-start | bytes 1048576 | tf_op jit(solution)/shard_map/all_to_all | solution.py:198
  47.7 10.3 %collective-permute-start.2 = (bf16[4,256]{1,0:T(4,128)(2,1)S(1)}, bf16[4,256]{1,0:T(4,128)(2,1)S(1)}, u32[]{:S(2)}, u32[]{:S(2)}) collective-permute-start(bf16[4,256]{1,0:T(4,128)(2,1)S(1)} %pad_maximum_fusion), channel_id=1, source_target_pairs={{0,2},{1,3},{2,0},{3,1},{4,6},{5,7},{6,4},{7,5},{8,10},{9,11},{10,... | collective-permute-start | bytes 6152 | tf_op jit(solution)/shard_map/ppermute | solution.py:175
  52.1 5.9 %collective-permute-start.1 = (bf16[256,256]{1,0:T(8,128)(2,1)S(1)}, bf16[256,256]{1,0:T(8,128)(2,1)S(1)}, u32[]{:S(2)}, u32[]{:S(2)}) collective-permute-start(bf16[256,256]{1,0:T(8,128)(2,1)S(1)} %reshape.11.y_ref), channel_id=1, source_target_pairs={{0,256},{256,0},{1,257},{257,1},{2,258},{258,2},{3,259},{259,3},{4... | collective-permute-start | bytes 393224 | tf_op jit(solution)/shard_map/ppermute | solution.py:199
